TPU v7x, 256 devices: a whole 4x4x8 slice. The times are simulated.
256 devices in a mesh: src: 16 (over y_hi, z), freq: 16 (over x, y_lo, core).
Axes of the slice: x: 4, y: 4 (y_hi: 2, y_lo: 2; y = y_hi * 2 + y_lo), z: 8, core: 2. Of those that a mesh axis runs over, the one named last changes fastest.
Arguments:
- reflection: bfloat16 [2, 64, 2304, 2304], P(None, 'freq', 'src'), may hold values from -0.09375 to 0.09375
- focusing: bfloat16 [2, 64, 2304, 128], P(None, 'freq', 'src'), may hold values from -6 to 6
- direct_field: float32 [128, 2304, 128], P('freq', 'src'), may hold values from -6 to 6
- onset_index: int32 [2304, 128], P('src'), may hold values from 1 to 63
- end_index: int32 [2304, 128], P('src'), may hold values from 65 to 127
Outputs:
- updated: float32 [128, 2304, 128], P('freq', 'src')
Inputs may be any that keep to these rules, and one draw needn't show every extreme that they name: `onset_index`: each trace's onset lies before the middle sample. `end_index`: each trace's window ends after the middle sample.
All inputs are finite; a program needn't handle non-finite values.
Results may differ from a plain program's by a relative error of at most 0.0003.
Values may be sent and summed in bfloat16 or wider, within the bound.
A program may use at most 64 MiB of HBM per device.

v0:
```python
import math

import jax
import jax.numpy as jnp
from jax import lax
from jax.sharding import PartitionSpec as P

HIGHEST = lax.Precision.HIGHEST


def reverse_bits(values, bit_count):
    result = jnp.zeros_like(values)
    for bit_index in range(bit_count):
        result = result + values // 2**bit_index % 2 * 2 ** (bit_count - 1 - bit_index)
    return result


def phase_tables(sample_rows, frequency, sample_total):
    phase_index = sample_rows[:, None] * frequency[None, :] % sample_total
    twiddle_angle = phase_index.astype(jnp.float32) * (2.0 * math.pi / sample_total)
    return (jnp.cos(twiddle_angle), jnp.sin(twiddle_angle))


def per_device(reflection, focusing, direct_field, onset_index, end_index):
    freqs_dev = reflection.shape[1]
    group_size = lax.axis_size("freq")
    bit_count = group_size.bit_length() - 1
    device_index = lax.axis_index("freq")
    freq_total = freqs_dev * group_size
    sample_total = 2 * freq_total
    block_samples = sample_total // group_size
    norm_factor = 1.0 / math.sqrt(freq_total)
    residue = reverse_bits(device_index, bit_count)
    frequency = jnp.arange(freqs_dev, dtype=jnp.int32) * group_size + residue
    block_piece = lax.all_gather(focusing, "src", axis=2, tiled=True)
    real_part = jnp.einsum(
        "lrs,lsn->lrn", reflection[0], block_piece[0], preferred_element_type=jnp.float32
    ) - jnp.einsum(
        "lrs,lsn->lrn", reflection[1], block_piece[1], preferred_element_type=jnp.float32
    )
    imag_part = jnp.einsum(
        "lrs,lsn->lrn", reflection[0], block_piece[1], preferred_element_type=jnp.float32
    ) + jnp.einsum(
        "lrs,lsn->lrn", reflection[1], block_piece[0], preferred_element_type=jnp.float32
    )
    spectrum = jnp.stack((real_part, imag_part))
    sample_rows = jnp.arange(block_samples * lax.axis_size("freq"), dtype=jnp.int32)
    cosine, sine_table = phase_tables(sample_rows, frequency, sample_total)
    reversed_trace = lax.psum_scatter(
        (
            jnp.einsum("tl,lrn->trn", cosine, spectrum[0], precision=HIGHEST)
            + jnp.einsum("tl,lrn->trn", sine_table, spectrum[1], precision=HIGHEST)
        )
        * norm_factor,
        "freq",
        scatter_dimension=0,
        tiled=True,
    )
    sample_rows = device_index * block_samples + jnp.arange(block_samples, dtype=jnp.int32)
    source_sample = (sample_total - sample_rows) % sample_total
    window = (source_sample[:, None, None] >= onset_index[None]) & (
        source_sample[:, None, None] < end_index[None]
    )
    return direct_field - jnp.where(window, reversed_trace, jnp.float32(0.0))


def solution(mesh):
    placed = (
        P(None, "freq", "src", None),
        P(None, "freq", "src", None),
        P("freq", "src", None),
        P("src", None),
        P("src", None),
    )
    return jax.shard_map(
        per_device, mesh=mesh, in_specs=placed, out_specs=P("freq", "src", None), check_vma=False
    )
```

profile of v0, /device:TPU:1, one launch (start us, length us, event | category | flops | bytes accessed | tf_op | source)
XLA Modules:
  0.0 261.0 jit_solution(13054473246820596416)
XLA Ops:
  6.5 0.0 all-gather.2.cloned.1.call-start
  6.5 0.7 all-gather.2.cloned.1.call-update
  7.3 0.0 reduce-scatter.2.cloned.1.call-start
  7.4 108.0 %all-gather.2.cloned.1.call-done = bf16[2,4,2304,128]{3,2,1,0:T(8,128)(2,1)} async-done(((bf16[2,4,144,128]{3,2,1,0:T(8,128)(2,1)}), bf16[2,4,2304,128]{3,2,1,0:T(8,128)(2,1)}) %all-gather.2.cloned.1.call-update) | async-done | bytes 4718608 | tf_op jit(solution)/shard_map/all_gather | solution.py:35
  115.3 0.0 copy-start.3
  115.4 3.5 %fusion.2 = f32[4,144,128]{2,1,0:T(8,128)S(1)} fusion(bf16[2,4,144,2304]{3,2,1,0:T(8,128)(2,1)} %param.5, bf16[2,4,2304,128]{3,2,1,0:T(8,128)(2,1)} %all-gather.2.cloned.1.call-done), kind=kOutput, calls=%fused_computation.3 | convolution fusion | flops 339738624 | bytes 5308416 | tf_op jit(solution)/shard_map/lrs,lsn->lrn/dot_general | solution.py:38
  118.8 0.5 copy-done.3
  119.4 0.0 slice-start
  119.4 2.7 %fusion.6 = f32[4,144,128]{2,1,0:T(8,128)S(1)} fusion(bf16[2,4,144,2304]{3,2,1,0:T(8,128)(2,1)S(1)} %copy-done.3, bf16[2,4,2304,128]{3,2,1,0:T(8,128)(2,1)} %all-gather.2.cloned.1.call-done), kind=kOutput, calls=%fused_computation.7 | convolution fusion | flops 339738624 | bytes 5308416 | tf_op jit(solution)/shard_map/lrs,lsn->lrn/dot_general | solution.py:36
  122.1 0.0 slice-start.1
  122.1 7.7 %fusion.13 = f32[128,144,128]{2,0,1:T(8,128)S(1)} fusion(f32[4,144,128]{2,1,0:T(8,128)S(1)} %fusion.2, f32[4,144,128]{2,1,0:T(8,128)S(1)} %fusion.6, s32[4]{0:T(128)S(1)} %multiply_add_fusion), kind=kOutput, calls=%fused_computation.19 | convolution fusion | flops 113327104 | bytes 10027024 | tf_op jit(solution)/shard_map/tl,lrn->trn/dot_general | solution.py:51
  129.8 0.0 slice-done
  129.8 0.0 slice-done.1
  129.8 0.9 fusion.4
  130.7 0.9 fusion
  131.6 11.0 %add_multiply_fusion = f32[128,144,128]{2,0,1:T(8,128)} fusion(f32[128,144,128]{2,0,1:T(8,128)S(1)} %fusion.13, f32[4,144,128]{2,1,0:T(8,128)S(1)} %fusion, f32[4,144,128]{2,1,0:T(8,128)S(1)} %fusion.4, s32[4]{0:T(128)S(1)} %multiply_add_fusion), kind=kOutput, calls=%fused_computation | convolution fusion | flops 118045696 | bytes 19464208 | tf_op jit(solution)/shard_map/tl,lrn->trn/dot_general | solution.py:52
  142.6 0.0 copy-start
  142.6 0.0 copy-start.1
  142.6 0.0 copy-start.2
  142.6 0.0 reduce-scatter.2.cloned.1.call-update
  142.6 109.2 %reduce-scatter.2.cloned.1.call-done = f32[8,144,128]{2,0,1:T(8,128)} async-done(((f32[128,144,128]{2,0,1:T(8,128)}), f32[8,144,128]{2,0,1:T(8,128)}) %reduce-scatter.2.cloned.1.call-update) | async-done | bytes 589840 | tf_op jit(solution)/shard_map/reduce_scatter | solution.py:49
  251.9 0.0 copy-done
  251.9 0.0 copy-done.1
  251.9 0.0 copy-done.2
  251.9 1.4 copy_subtract_fusion
  253.2 0.9 copy.7
  (3 shorter events, 0.0 us)
Async XLA Ops:
  6.5 108.8 %all-gather.2.cloned.1.call-start = ((), (), s32[]{:S(2)}) async-start(), calls=%async_computation.1 | async-start | bytes 5013504 | tf_op jit(solution)/shard_map/all_gather | solution.py:35
  7.3 244.6 %reduce-scatter.2.cloned.1.call-start = ((), (), s32[]{:S(2)}) async-start(), calls=%async_computation.2 | async-start | bytes 10027008 | tf_op jit(solution)/shard_map/reduce_scatter | solution.py:49
  115.3 4.0 %copy-start.3 = (bf16[2,4,144,2304]{3,2,1,0:T(8,128)(2,1)S(1)}, bf16[2,4,144,2304]{3,2,1,0:T(8,128)(2,1)}, u32[]{:S(2)}) copy-start(bf16[2,4,144,2304]{3,2,1,0:T(8,128)(2,1)} %param.5) | copy-start | bytes 15925252
  119.4 10.4 %slice-start = ((s8[4718592]{0:T(1024)(128)(4,1)}), s8[4194304]{0:T(1024)(128)(4,1)S(1)}, s32[]{:S(2)}) async-start(s8[4718592]{0:T(1024)(128)(4,1)} %bitcast.24), calls=%async_computation.3 | async-start | bytes 8388608
  122.1 7.7 %slice-start.1 = ((s8[4718592]{0:T(1024)(128)(4,1)}), s8[524288]{0:T(1024)(128)(4,1)S(1)}, s32[]{:S(2)}) async-start(s8[4718592]{0:T(1024)(128)(4,1)} %bitcast.24), calls=%async_computation.4 | async-start | bytes 1048576
  142.6 109.3 %copy-start = (f32[8,144,128]{2,1,0:T(8,128)S(1)}, f32[8,144,128]{2,1,0:T(8,128)}, u32[]{:S(2)}) copy-start(f32[8,144,128]{2,1,0:T(8,128)} %param.7) | copy-start | bytes 1769476
  142.6 109.3 %copy-start.1 = (s32[144,128]{1,0:T(8,128)S(1)}, s32[144,128]{1,0:T(8,128)}, u32[]{:S(2)}) copy-start(s32[144,128]{1,0:T(8,128)} %param.9) | copy-start | bytes 221188
  142.6 109.3 %copy-start.2 = (s32[144,128]{1,0:T(8,128)S(1)}, s32[144,128]{1,0:T(8,128)}, u32[]{:S(2)}) copy-start(s32[144,128]{1,0:T(8,128)} %param.8) | copy-start | bytes 221188
Sparse Core Ops, SparseCore 0:
  10.1 105.2 all-gather.1
  142.7 109.0 reduce-scatter.1
where the time goes:
time: 261 us
  waiting for transfers between devices  218 us (84%)
  matrix products  26.6 us (10%)
  between operations  13.6 us (5%)
    reduce_scatter x1, waiting for transfers between devices, per_device(): lax.psum_scatter((jnp.einsum('tl,lrn->trn', cosine, spectrum[0], precisio...  109 us
    all_gather x1, waiting for transfers between devices, per_device(): block_piece = lax.all_gather(focusing, 'src', axis=2, tiled=True)  108 us
    dot_general x1, matrix products, per_device(): jnp.einsum('tl,lrn->trn', sine_table, spectrum[1], precision=HIGHEST)  11 us
    dot_general x1, matrix products, per_device(): jnp.einsum('tl,lrn->trn', cosine, spectrum[0], precision=HIGHEST)  7.7 us
  transfers between devices with their start and end apart: 2, of which 2 were waited for; matrix products, arithmetic and copies ran while one was open for 0% of the time, Pallas kernels for 0%

commit v1 on v0

v1 whole, which is shorter than its diff:
```python
import functools

import jax
import jax.numpy as jnp
import numpy as np
from jax import lax
from jax.experimental import pallas as pl
from jax.experimental.pallas import tpu as pltpu
from jax.sharding import PartitionSpec as P

MESH = pl.DeviceIdType.MESH

Z = 8
SRC = 16
FRQ = 16
L = 4
ROWS = 144
NPTS = 128
NSRC = SRC * ROWS
PER = ROWS // FRQ
PIECE = 24
BACK = PER * 8

A, B, ALL = (0, 128), (128, 128), (0, 256)
OWN, PAR = 0, 1
MOVES = (
    ("z+", OWN, -1, ALL),
    ("z+", OWN, -2, ALL),
    ("z+", OWN, -3, ALL),
    ("z+", OWN, -4, A),
    ("z+", PAR, -2, ALL),
    ("z+", PAR, -3, A),
    ("z-", OWN, 1, ALL),
    ("z-", OWN, 2, ALL),
    ("z-", OWN, 3, ALL),
    ("z-", OWN, 4, B),
    ("z-", PAR, 2, ALL),
    ("z-", PAR, 3, A),
    ("y", PAR, 0, ALL),
    ("y", PAR, -1, ALL),
    ("y", PAR, 1, ALL),
    ("y", PAR, -3, B),
    ("y", PAR, 3, B),
    ("y", PAR, 4, ALL),
)
ZP1, ZP2, ZP3, ZP4, ZQ2, ZQ3, ZM1, ZM2, ZM3, ZM4, ZN2, ZN3, Y0, YM1, YP1, YM3, YP3, Y4 = range(18)


def split(value):
    high = value.astype(jnp.bfloat16)
    return high, (value - high.astype(jnp.float32)).astype(jnp.bfloat16)


def kernel(
    refl, focus, direct, onset, ending, table,
    out,
    gath, mat, spec, got, trace, back, dir_v, on_v, end_v, tab_v, tab3, out_v,
    g_send, g_recv, s_send, s_recv, t_send, t_recv, f_sem, r_sem, loc_sem, own_sem, out_sem,
):
    s_me, f_me = lax.axis_index("src"), lax.axis_index("freq")
    h, z = s_me // Z, lax.rem(s_me, Z)
    targets = {
        "z+": {"src": h * Z + lax.rem(z + 1, Z), "freq": f_me},
        "z-": {"src": h * Z + lax.rem(z + Z - 1, Z), "freq": f_me},
        "y": {"src": (1 - h) * Z + z, "freq": f_me},
    }

    def peer(d):
        return lax.rem(f_me + d, FRQ)

    def rows_of(half, offset):
        hh = h if half == OWN else 1 - h
        block = hh * Z + lax.rem(z + offset + Z, Z)
        return pl.ds(pl.multiple_of(block * ROWS, 16), ROWS)

    def move(k, l, receiving):
        way, half, offset, (lane, width) = MOVES[k]
        if not receiving:
            if way == "y":
                half = 1 - half
            else:
                offset = offset + (1 if way == "z+" else -1)
        ref = gath.at[l, rows_of(half, offset), pl.ds(lane, width)]
        return pltpu.make_async_remote_copy(
            src_ref=ref, dst_ref=ref, send_sem=g_send.at[l, k], recv_sem=g_recv.at[l, k],
            device_id=targets[way], device_id_type=MESH,
        )

    def send(k, l):
        move(k, l, False).start()

    def arrived(k, l):
        move(k, l, True).wait_recv()

    mine = pl.ds(pl.multiple_of(s_me * ROWS, 16), ROWS)

    def focus_copy(part, l):
        return pltpu.make_async_copy(
            focus.at[part, l], gath.at[l, mine, pl.ds(part * NPTS, NPTS)], f_sem.at[part, l]
        )

    def refl_copy(part, l):
        return pltpu.make_async_copy(
            refl.at[part, l], mat.at[l, pl.ds(part * ROWS, ROWS)], r_sem.at[part, l]
        )

    others = [
        pltpu.make_async_copy(a, b, loc_sem.at[i])
        for i, (a, b) in enumerate(((table, tab_v), (onset, on_v), (ending, end_v), (direct, dir_v)))
    ]
    for l in range(L):
        for part in range(2):
            focus_copy(part, l).start()

    barrier = pltpu.get_barrier_semaphore()
    for way in ("z+", "z-", "y"):
        pl.semaphore_signal(barrier, inc=1, device_id=targets[way], device_id_type=MESH)
    for d in range(1, FRQ):
        pl.semaphore_signal(
            barrier, inc=1, device_id={"src": s_me, "freq": peer(d)}, device_id_type=MESH
        )
    for l in range(L):
        for part in range(2):
            refl_copy(part, l).start()
    for c in others:
        c.start()
    for l in range(L):
        for part in range(2):
            focus_copy(part, l).wait()
    pl.semaphore_wait(barrier, 3 + FRQ - 1)

    def phase(body):
        def step(l, carry):
            body(l)
            return carry

        lax.fori_loop(0, L, step, 0)

    def start_own(l):
        send(ZP1, l)
        send(ZM1, l)
        send(Y0, l)

    def near(l):
        arrived(ZP1, l)
        send(ZP2, l)
        send(YM1, l)
        arrived(ZM1, l)
        send(ZM2, l)
        send(YP1, l)

    def second(l):
        arrived(ZP2, l)
        send(ZP3, l)
        arrived(ZM2, l)
        send(ZM3, l)

    def third(l):
        arrived(ZP3, l)
        send(ZP4, l)
        send(YM3, l)
        arrived(ZM3, l)
        send(ZM4, l)
        send(YP3, l)
        arrived(YM1, l)
        send(ZQ2, l)
        arrived(YP1, l)
        send(ZN2, l)

    def fourth(l):
        arrived(ZP4, l)
        arrived(ZM4, l)
        send(Y4, l)
        arrived(ZQ2, l)
        send(ZQ3, l)
        arrived(ZN2, l)
        send(ZN3, l)

    def piece_copy(d, l, receiving):
        to = peer(d)
        place = peer(FRQ - d) if receiving else f_me
        return pltpu.make_async_remote_copy(
            src_ref=spec.at[l, pl.ds(pl.multiple_of(to * PIECE, 8), PIECE)],
            dst_ref=got.at[l, pl.ds(pl.multiple_of(place * PIECE, 8), PIECE)],
            send_sem=s_send.at[l, d], recv_sem=s_recv.at[l, d],
            device_id={"src": s_me, "freq": to}, device_id_type=MESH,
        )

    def own_piece(l):
        rows = pl.ds(pl.multiple_of(f_me * PIECE, 8), PIECE)
        return pltpu.make_async_copy(spec.at[l, rows], got.at[l, rows], own_sem.at[l])

    def product(l):
        for k in (Y0, YM3, YP3, ZQ3, ZN3, Y4):
            arrived(k, l)
        for part in range(2):
            refl_copy(part, l).wait()
        both = jnp.dot(mat[l], gath[l], preferred_element_type=jnp.float32)
        re = both[:ROWS, :NPTS] - both[ROWS:, NPTS:]
        im = both[:ROWS, NPTS:] + both[ROWS:, :NPTS]
        for part, value in enumerate((re, im)):
            for j in range(PER):
                for p in (0, 8):
                    spec[l, pl.ds(p * PIECE + part * PER + j, 8, stride=PIECE), :] = value[
                        16 * j + p : 16 * j + p + 8
                    ]
        own_piece(l).start()
        for d in range(1, FRQ):
            piece_copy(d, l, False).start()

    phase(start_own)
    phase(near)
    phase(second)
    phase(third)
    phase(fourth)
    for c in others:
        c.wait()
    high, low = split(tab_v[...])
    tab3[...] = jnp.concatenate([high, high, low], axis=1)
    phase(product)

    def collect(l):
        own_piece(l).wait()
        for d in range(1, FRQ):
            piece_copy(d, l, True).wait_recv()

    phase(collect)
    for j in range(PER):
        cols = jnp.concatenate(
            [
                got[l, pl.ds(part * PER + j, FRQ, stride=PIECE), :]
                for l in range(L)
                for part in range(2)
            ],
            axis=0,
        )
        high, low = split(cols)
        result = jnp.dot(
            tab3[...],
            jnp.concatenate([high, low, high], axis=0),
            preferred_element_type=jnp.float32,
        )
        for d in range(FRQ):
            trace[pl.ds(d * BACK + j * 8, 8), :] = result[8 * d : 8 * d + 8]

    def back_copy(d, receiving):
        to = peer(d)
        place = peer(FRQ - d) if receiving else f_me
        return pltpu.make_async_remote_copy(
            src_ref=trace.at[pl.ds(pl.multiple_of(to * BACK, 8), BACK)],
            dst_ref=back.at[pl.ds(pl.multiple_of(place * BACK, 8), BACK)],
            send_sem=t_send.at[d], recv_sem=t_recv.at[d],
            device_id={"src": s_me, "freq": to}, device_id_type=MESH,
        )

    rows = pl.ds(pl.multiple_of(f_me * BACK, 8), BACK)
    own_back = pltpu.make_async_copy(trace.at[rows], back.at[rows], own_sem.at[L])
    for d in range(1, FRQ):
        back_copy(d, False).start()
    own_back.start()
    own_back.wait()
    for d in range(1, FRQ):
        back_copy(d, True).wait_recv()

    def out_copy(t):
        return pltpu.make_async_copy(out_v.at[t], out.at[t], out_sem.at[t])

    for t in range(8):
        sample = lax.rem(128 - (8 * f_me + t), 128)
        for j in range(PER):
            for p in (0, 8):
                r = pl.ds(16 * j + p, 8)
                value = back[pl.ds(p * BACK + j * 8 + t, 8, stride=BACK), :]
                window = (sample >= on_v[r, :]) & (sample < end_v[r, :])
                out_v[t, r, :] = dir_v[t, r, :] - jnp.where(window, value, 0.0)
        out_copy(t).start()

    def sent(l):
        for k in range(len(MOVES)):
            move(k, l, False).wait_send()
        for d in range(1, FRQ):
            piece_copy(d, l, False).wait_send()

    phase(sent)
    for d in range(1, FRQ):
        back_copy(d, False).wait_send()
    for t in range(8):
        out_copy(t).wait()


def transform_table():
    device = np.arange(FRQ)
    reverse = sum(((device >> b) & 1) << (3 - b) for b in range(4))
    frequency = (np.arange(L)[:, None] * FRQ + reverse[None, :]).astype(np.int64)
    angle = (np.arange(128)[:, None, None] * frequency[None]) % 128 * (2.0 * np.pi / 128)
    full = np.stack([np.cos(angle), np.sin(angle)], axis=2).reshape(128, 128) / 8.0
    return full.astype(np.float32)


def per_device(reflection, focusing, direct_field, onset_index, end_index):
    f32, bf16 = jnp.float32, jnp.bfloat16
    dma = pltpu.SemaphoreType.DMA
    hbm = pl.BlockSpec(memory_space=pltpu.HBM)
    return pl.pallas_call(
        kernel,
        out_shape=jax.ShapeDtypeStruct((8, ROWS, NPTS), f32),
        in_specs=[hbm] * 6,
        out_specs=hbm,
        scratch_shapes=[
            pltpu.VMEM((L, NSRC, 2 * NPTS), bf16),
            pltpu.VMEM((L, 2 * ROWS, NSRC), bf16),
            pltpu.VMEM((L, FRQ * PIECE, NPTS), f32),
            pltpu.VMEM((L, FRQ * PIECE, NPTS), f32),
            pltpu.VMEM((FRQ * BACK, NPTS), f32),
            pltpu.VMEM((FRQ * BACK, NPTS), f32),
            pltpu.VMEM((8, ROWS, NPTS), f32),
            pltpu.VMEM((ROWS, NPTS), jnp.int32),
            pltpu.VMEM((ROWS, NPTS), jnp.int32),
            pltpu.VMEM((128, 128), f32),
            pltpu.VMEM((128, 384), bf16),
            pltpu.VMEM((8, ROWS, NPTS), f32),
            dma((L, len(MOVES))),
            dma((L, len(MOVES))),
            dma((L, FRQ)),
            dma((L, FRQ)),
            dma((FRQ,)),
            dma((FRQ,)),
            dma((2, L)),
            dma((2, L)),
            dma((4,)),
            dma((L + 1,)),
            dma((8,)),
        ],
        compiler_params=pltpu.CompilerParams(
            collective_id=0, has_side_effects=True, vmem_limit_bytes=63 * 2**20
        ),
        name="marchenko",
    )(
        reflection, focusing, direct_field, onset_index, end_index,
        jnp.asarray(transform_table()),
    )


def solution(mesh):
    placed = (
        P(None, "freq", "src", None),
        P(None, "freq", "src", None),
        P("freq", "src", None),
        P("src", None),
        P("src", None),
    )
    return jax.shard_map(
        per_device, mesh=mesh, in_specs=placed, out_specs=P("freq", "src", None), check_vma=False
    )
```

time: 261 us -> 67.5 us (0.26)
  waiting for transfers between devices: 218 us -> 0 us
  Pallas kernels: 0 us -> 65.4 us
  matrix products: 26.6 us -> 0 us
  between operations: 13.6 us -> 0.01 us
    reduce_scatter x1 -> x0, waiting for transfers between devices: 109 us -> none  [per_device(): lax.psum_scatter((jnp.einsum('tl,lrn->trn', cosine, spectrum[0], precisio...]
    all_gather x1 -> x0, waiting for transfers between devices: 108 us -> none  [per_device(): block_piece = lax.all_gather(focusing, 'src', axis=2, tiled=True)]
    pallas_call x0 -> x1, Pallas kernels: none -> 65.4 us  [per_device(): pl.pallas_call(kernel, out_shape=jax.ShapeDtypeStruct((8, ROWS, NPTS), f3...]
    dot_general x6 -> x0, matrix products: 26.6 us -> none  [the longest x1 11 us: per_device(): jnp.einsum('tl,lrn->trn', sine_table, spectrum[1], precision=HIGHEST)]
  transfers between devices with their start and end apart: 2 -> 0, of which waited for: 2 -> 0; matrix products, arithmetic and copies ran while one was open for 0% -> 0% of each run, Pallas kernels for 0% -> 0%
where the time goes in v1:
time: 67.5 us; the launch traced here: 67.3 us
  Pallas kernels  65.4 us (97%)
  local copies, waits for them, and re-layouts  1.92 us (3%)
    pallas_call x1, Pallas kernels, per_device(): pl.pallas_call(kernel, out_shape=jax.ShapeDtypeStruct((8, ROWS, NPTS), f3...  65.4 us
    unnamed x1, local copies, waits for them, and re-layouts  1.92 us

profile of v1, /device:TPU:1, one launch (start us, length us, event | category | flops | bytes accessed | tf_op | source)
XLA Modules:
  0.0 67.3 jit_solution(12467854447991678859)
XLA Ops:
  0.0 65.4 %marchenko.1 = f32[8,144,128]{2,1,0:T(8,128)} custom-call(bf16[2,4,144,2304]{3,2,1,0:T(8,128)(2,1)} %refl.1, bf16[2,4,144,128]{3,2,1,0:T(8,128)(2,1)} %focus.1, f32[8,144,128]{2,1,0:T(8,128)} %direct.1, s32[144,128]{1,0:T(8,128)} %onset.1, s32[144,128]{1,0:T(8,128)} %ending.1, f32[128,128]{1,0:T(8,128)} %constant.2.clone.table), custom_call_target="tpu_custom_call" | custom-call | tf_op jit(solution)/shard_map/marchenko/pallas_call | solution.py:304
  65.4 1.9 %copy.8 = f32[8,144,128]{2,1,0:T(8,128)} copy(f32[8,144,128]{2,1,0:T(8,128)} %marchenko.1) | data formatting | bytes 1179648

commit v2 on v1

--- a/solution.py
+++ b/solution.py
@@ -2,6 +2,7 @@
 
 import jax
 import jax.numpy as jnp
+import ml_dtypes
 import numpy as np
 from jax import lax
 from jax.experimental import pallas as pl
@@ -19,6 +20,7 @@
 NSRC = SRC * ROWS
 PER = ROWS // FRQ
 PIECE = 24
+LAG = 3
 BACK = PER * 8
 
 A, B, ALL = (0, 128), (128, 128), (0, 256)
@@ -54,8 +56,8 @@
 def kernel(
     refl, focus, direct, onset, ending, table,
     out,
-    gath, mat, spec, got, trace, back, dir_v, on_v, end_v, tab_v, tab3, out_v,
-    g_send, g_recv, s_send, s_recv, t_send, t_recv, f_sem, r_sem, loc_sem, own_sem, out_sem,
+    gath, mat, spec, got, trace, back, dir_v, on_v, end_v, tab_v, tab_a, tab_b, early,
+    g_send, g_recv, s_send, s_recv, t_send, t_recv, f_sem, r_sem, loc_sem, own_sem,
 ):
     s_me, f_me = lax.axis_index("src"), lax.axis_index("freq")
     h, z = s_me // Z, lax.rem(s_me, Z)
@@ -180,14 +182,14 @@
         to = peer(d)
         place = peer(FRQ - d) if receiving else f_me
         return pltpu.make_async_remote_copy(
-            src_ref=spec.at[l, pl.ds(pl.multiple_of(to * PIECE, 8), PIECE)],
-            dst_ref=got.at[l, pl.ds(pl.multiple_of(place * PIECE, 8), PIECE)],
+            src_ref=spec.at[l, pl.ds(pl.multiple_of(to * PIECE, 8), 2 * PER)],
+            dst_ref=got.at[l, pl.ds(pl.multiple_of(place * PIECE, 8), 2 * PER)],
             send_sem=s_send.at[l, d], recv_sem=s_recv.at[l, d],
             device_id={"src": s_me, "freq": to}, device_id_type=MESH,
         )
 
     def own_piece(l):
-        rows = pl.ds(pl.multiple_of(f_me * PIECE, 8), PIECE)
+        rows = pl.ds(pl.multiple_of(f_me * PIECE, 8), 2 * PER)
         return pltpu.make_async_copy(spec.at[l, rows], got.at[l, rows], own_sem.at[l])
 
     def product(l):
@@ -212,36 +214,56 @@
     phase(near)
     phase(second)
     phase(third)
-    phase(fourth)
     for c in others:
         c.wait()
-    high, low = split(tab_v[...])
-    tab3[...] = jnp.concatenate([high, high, low], axis=1)
-    phase(product)
+    tab_a[...] = tab_v[:, :384].astype(jnp.bfloat16)
+    tab_b[...] = tab_v[:, 384:].astype(jnp.bfloat16)
+
+    def last(i, carry):
+        @pl.when(i < L)
+        def _():
+            fourth(i)
+
+        @pl.when(i >= LAG)
+        def _():
+            product(i - LAG)
+
+        return carry
+
+    lax.fori_loop(0, L + LAG, last, 0)
 
     def collect(l):
         own_piece(l).wait()
         for d in range(1, FRQ):
             piece_copy(d, l, True).wait_recv()
 
-    phase(collect)
-    for j in range(PER):
+    def columns(j, l):
+        high, low = split(
+            jnp.concatenate(
+                [got[l, pl.ds(part * PER + j, FRQ, stride=PIECE), :] for part in range(2)], axis=0
+            )
+        )
+        return jnp.concatenate([high, low, high], axis=0)
+
+    def transform(tab, j, ls):
+        js = range(j, min(j + 2, PER))
         cols = jnp.concatenate(
-            [
-                got[l, pl.ds(part * PER + j, FRQ, stride=PIECE), :]
-                for l in range(L)
-                for part in range(2)
-            ],
-            axis=0,
-        )
-        high, low = split(cols)
-        result = jnp.dot(
-            tab3[...],
-            jnp.concatenate([high, low, high], axis=0),
-            preferred_element_type=jnp.float32,
-        )
-        for d in range(FRQ):
-            trace[pl.ds(d * BACK + j * 8, 8), :] = result[8 * d : 8 * d + 8]
+            [jnp.concatenate([columns(k, l) for l in ls], axis=0) for k in js], axis=1
+        )
+        result = jnp.dot(tab, cols, preferred_element_type=jnp.float32)
+        return [(k, result[:, NPTS * i : NPTS * (i + 1)]) for i, k in enumerate(js)]
+
+    for l in range(L - 1):
+        collect(l)
+    for j in range(0, PER, 2):
+        for k, result in transform(tab_a[:, : 96 * (L - 1)], j, range(L - 1)):
+            early[k] = result
+    collect(L - 1)
+    for j in range(0, PER, 2):
+        for k, result in transform(tab_b[:, :96], j, (L - 1,)):
+            result = result + early[k]
+            for d in range(FRQ):
+                trace[pl.ds(d * BACK + k * 8, 8), :] = result[8 * d : 8 * d + 8]
 
     def back_copy(d, receiving):
         to = peer(d)
@@ -262,9 +284,6 @@
     for d in range(1, FRQ):
         back_copy(d, True).wait_recv()
 
-    def out_copy(t):
-        return pltpu.make_async_copy(out_v.at[t], out.at[t], out_sem.at[t])
-
     for t in range(8):
         sample = lax.rem(128 - (8 * f_me + t), 128)
         for j in range(PER):
@@ -272,8 +291,7 @@
                 r = pl.ds(16 * j + p, 8)
                 value = back[pl.ds(p * BACK + j * 8 + t, 8, stride=BACK), :]
                 window = (sample >= on_v[r, :]) & (sample < end_v[r, :])
-                out_v[t, r, :] = dir_v[t, r, :] - jnp.where(window, value, 0.0)
-        out_copy(t).start()
+                out[t, r, :] = dir_v[t, r, :] - jnp.where(window, value, 0.0)
 
     def sent(l):
         for k in range(len(MOVES)):
@@ -284,8 +302,6 @@
     phase(sent)
     for d in range(1, FRQ):
         back_copy(d, False).wait_send()
-    for t in range(8):
-        out_copy(t).wait()
 
 
 def transform_table():
@@ -293,8 +309,15 @@
     reverse = sum(((device >> b) & 1) << (3 - b) for b in range(4))
     frequency = (np.arange(L)[:, None] * FRQ + reverse[None, :]).astype(np.int64)
     angle = (np.arange(128)[:, None, None] * frequency[None]) % 128 * (2.0 * np.pi / 128)
-    full = np.stack([np.cos(angle), np.sin(angle)], axis=2).reshape(128, 128) / 8.0
-    return full.astype(np.float32)
+    full = np.stack([np.cos(angle), np.sin(angle)], axis=2).reshape(128, L, 32) / 8.0
+    full = full.astype(np.float32)
+    high = full.astype(ml_dtypes.bfloat16).astype(np.float32)
+    low = (full - high).astype(ml_dtypes.bfloat16).astype(np.float32)
+    three = np.concatenate([high, high, low], axis=2)
+    table = np.zeros((128, 512), np.float32)
+    table[:, : 96 * (L - 1)] = three[:, : L - 1].reshape(128, 96 * (L - 1))
+    table[:, 384:480] = three[:, L - 1]
+    return table
 
 
 def per_device(reflection, focusing, direct_field, onset_index, end_index):
@@ -303,9 +326,9 @@
     hbm = pl.BlockSpec(memory_space=pltpu.HBM)
     return pl.pallas_call(
         kernel,
-        out_shape=jax.ShapeDtypeStruct((8, ROWS, NPTS), f32),
+        out_shape=pltpu.VMEM((8, ROWS, NPTS), f32),
         in_specs=[hbm] * 6,
-        out_specs=hbm,
+        out_specs=pl.BlockSpec(memory_space=pltpu.VMEM),
         scratch_shapes=[
             pltpu.VMEM((L, NSRC, 2 * NPTS), bf16),
             pltpu.VMEM((L, 2 * ROWS, NSRC), bf16),
@@ -316,9 +339,10 @@
             pltpu.VMEM((8, ROWS, NPTS), f32),
             pltpu.VMEM((ROWS, NPTS), jnp.int32),
             pltpu.VMEM((ROWS, NPTS), jnp.int32),
-            pltpu.VMEM((128, 128), f32),
+            pltpu.VMEM((128, 512), f32),
             pltpu.VMEM((128, 384), bf16),
-            pltpu.VMEM((8, ROWS, NPTS), f32),
+            pltpu.VMEM((128, 128), bf16),
+            pltpu.VMEM((PER, 128, NPTS), f32),
             dma((L, len(MOVES))),
             dma((L, len(MOVES))),
             dma((L, FRQ)),
@@ -329,10 +353,9 @@
             dma((2, L)),
             dma((4,)),
             dma((L + 1,)),
-            dma((8,)),
         ],
         compiler_params=pltpu.CompilerParams(
-            collective_id=0, has_side_effects=True, vmem_limit_bytes=63 * 2**20
+            collective_id=0, has_side_effects=True, vmem_limit_bytes=60 * 2**20
         ),
         name="marchenko",
     )(

time: 67.5 us -> 63.5 us (0.941)
  Pallas kernels: 65.4 us -> 62.6 us
  local copies, waits for them, and re-layouts: 1.92 us -> 0.82 us
    pallas_call x1, Pallas kernels: 65.4 us -> 62.6 us  [per_device(): pl.pallas_call(kernel, out_shape=pltpu.VMEM((8, ROWS, NPTS), f32), in_spe...]
    unnamed x1, local copies, waits for them, and re-layouts: 1.92 us -> 0.82 us
where the time goes in v2:
time: 63.5 us
  Pallas kernels  62.6 us (99%)
  local copies, waits for them, and re-layouts  0.82 us (1%)
    pallas_call x1, Pallas kernels, per_device(): pl.pallas_call(kernel, out_shape=pltpu.VMEM((8, ROWS, NPTS), f32), in_spe...  62.6 us

profile of v2, /device:TPU:1, one launch (start us, length us, event | category | flops | bytes accessed | tf_op | source)
XLA Modules:
  0.0 63.5 jit_solution(17693400005120518531)
XLA Ops:
  0.0 62.6 %marchenko.1 = f32[8,144,128]{2,1,0:T(8,128)S(1)} custom-call(bf16[2,4,144,2304]{3,2,1,0:T(8,128)(2,1)} %refl.1, bf16[2,4,144,128]{3,2,1,0:T(8,128)(2,1)} %focus.1, f32[8,144,128]{2,1,0:T(8,128)} %direct.1, s32[144,128]{1,0:T(8,128)} %onset.1, s32[144,128]{1,0:T(8,128)} %ending.1, f32[128,512]{1,0:T(8,128)} %constant.2.clone.table), custom_call_target="tpu_custom_call" | custom-call | tf_op jit(solution)/shard_map/marchenko/pallas_call | solution.py:327
  62.6 0.8 %copy.8 = f32[8,144,128]{2,1,0:T(8,128)} copy(f32[8,144,128]{2,1,0:T(8,128)S(1)} %marchenko.1) | data formatting | bytes 1179648

commit v3 on v2

--- a/solution.py
+++ b/solution.py
@@ -20,8 +20,9 @@
 NSRC = SRC * ROWS
 PER = ROWS // FRQ
 PIECE = 24
+USED = PER + 1
 LAG = 3
-BACK = PER * 8
+BACK = (PER + 1) // 2 * 8
 
 A, B, ALL = (0, 128), (128, 128), (0, 256)
 OWN, PAR = 0, 1
@@ -53,6 +54,33 @@
     return high, (value - high.astype(jnp.float32)).astype(jnp.bfloat16)
 
 
+def block_scale(largest):
+    code = jnp.ceil(jnp.log2(jnp.maximum(largest, 2.0**-126)) * 16.0)
+    half = jnp.exp2(code * (-1.0 / 32))
+    return code.astype(jnp.int32), half, half * 32700.0
+
+
+def scale_of(code):
+    half = jnp.exp2(code.astype(jnp.float32) * (1.0 / 32))
+    return half, half * (1.0 / 32700)
+
+
+def to_int(value, scale):
+    return jnp.floor(value * scale[0] * scale[1] + 0.5).astype(jnp.int32)
+
+
+def pack(first, second):
+    return (first << 16) | (second & 0xFFFF)
+
+
+def first_of(word):
+    return word >> 16
+
+
+def second_of(word):
+    return (word << 16) >> 16
+
+
 def kernel(
     refl, focus, direct, onset, ending, table,
     out,
@@ -182,14 +210,14 @@
         to = peer(d)
         place = peer(FRQ - d) if receiving else f_me
         return pltpu.make_async_remote_copy(
-            src_ref=spec.at[l, pl.ds(pl.multiple_of(to * PIECE, 8), 2 * PER)],
-            dst_ref=got.at[l, pl.ds(pl.multiple_of(place * PIECE, 8), 2 * PER)],
+            src_ref=spec.at[l, pl.ds(pl.multiple_of(to * PIECE, 8), USED)],
+            dst_ref=got.at[l, pl.ds(pl.multiple_of(place * PIECE, 8), USED)],
             send_sem=s_send.at[l, d], recv_sem=s_recv.at[l, d],
             device_id={"src": s_me, "freq": to}, device_id_type=MESH,
         )
 
     def own_piece(l):
-        rows = pl.ds(pl.multiple_of(f_me * PIECE, 8), 2 * PER)
+        rows = pl.ds(pl.multiple_of(f_me * PIECE, 8), USED)
         return pltpu.make_async_copy(spec.at[l, rows], got.at[l, rows], own_sem.at[l])
 
     def product(l):
@@ -200,12 +228,15 @@
         both = jnp.dot(mat[l], gath[l], preferred_element_type=jnp.float32)
         re = both[:ROWS, :NPTS] - both[ROWS:, NPTS:]
         im = both[:ROWS, NPTS:] + both[ROWS:, :NPTS]
-        for part, value in enumerate((re, im)):
-            for j in range(PER):
-                for p in (0, 8):
-                    spec[l, pl.ds(p * PIECE + part * PER + j, 8, stride=PIECE), :] = value[
-                        16 * j + p : 16 * j + p + 8
-                    ]
+        for p in (0, 8):
+            rows = [slice(16 * j + p, 16 * j + p + 8) for j in range(PER)]
+            largest = functools.reduce(
+                jnp.maximum, [jnp.maximum(jnp.abs(re[r]), jnp.abs(im[r])) for r in rows]
+            )
+            code, *scale = block_scale(largest)
+            words = [pack(to_int(re[r], scale), to_int(im[r], scale)) for r in rows]
+            for j, word in enumerate(words + [code]):
+                spec[l, pl.ds(p * PIECE + j, 8, stride=PIECE), :] = word
         own_piece(l).start()
         for d in range(1, FRQ):
             piece_copy(d, l, False).start()
@@ -238,9 +269,11 @@
             piece_copy(d, l, True).wait_recv()
 
     def columns(j, l):
+        word = got[l, pl.ds(j, FRQ, stride=PIECE), :]
+        one, two = scale_of(got[l, pl.ds(PER, FRQ, stride=PIECE), :])
         high, low = split(
             jnp.concatenate(
-                [got[l, pl.ds(part * PER + j, FRQ, stride=PIECE), :] for part in range(2)], axis=0
+                [part(word).astype(jnp.float32) * one * two for part in (first_of, second_of)], axis=0
             )
         )
         return jnp.concatenate([high, low, high], axis=0)
@@ -258,12 +291,23 @@
     for j in range(0, PER, 2):
         for k, result in transform(tab_a[:, : 96 * (L - 1)], j, range(L - 1)):
             early[k] = result
+    sample = lax.rem(128 - lax.broadcasted_iota(jnp.int32, (128, NPTS), 0), 128)
     collect(L - 1)
+    largest = jnp.zeros((128, NPTS), jnp.float32)
     for j in range(0, PER, 2):
         for k, result in transform(tab_b[:, :96], j, (L - 1,)):
-            result = result + early[k]
-            for d in range(FRQ):
-                trace[pl.ds(d * BACK + k * 8, 8), :] = result[8 * d : 8 * d + 8]
+            r = pl.ds(16 * k + f_me, 1)
+            window = (sample >= on_v[r, :]) & (sample < end_v[r, :])
+            result = jnp.where(window, result + early[k], 0.0)
+            early[k] = result
+            largest = jnp.maximum(largest, jnp.abs(result))
+    code, *scale = block_scale(largest)
+    for j in range(0, PER, 2):
+        word = pack(
+            to_int(early[j], scale), to_int(early[j + 1], scale) if j + 1 < PER else code
+        )
+        for d in range(FRQ):
+            trace[pl.ds(d * BACK + j * 4, 8), :] = word[8 * d : 8 * d + 8]
 
     def back_copy(d, receiving):
         to = peer(d)
@@ -285,13 +329,15 @@
         back_copy(d, True).wait_recv()
 
     for t in range(8):
-        sample = lax.rem(128 - (8 * f_me + t), 128)
-        for j in range(PER):
-            for p in (0, 8):
+        for p in (0, 8):
+            words = [
+                back[pl.ds(p * BACK + i * 8 + t, 8, stride=BACK), :] for i in range((PER + 1) // 2)
+            ]
+            one, two = scale_of(second_of(words[-1]))
+            for j in range(PER):
+                value = (first_of, second_of)[j % 2](words[j // 2]).astype(jnp.float32)
                 r = pl.ds(16 * j + p, 8)
-                value = back[pl.ds(p * BACK + j * 8 + t, 8, stride=BACK), :]
-                window = (sample >= on_v[r, :]) & (sample < end_v[r, :])
-                out[t, r, :] = dir_v[t, r, :] - jnp.where(window, value, 0.0)
+                out[t, r, :] = dir_v[t, r, :] - value * one * two
 
     def sent(l):
         for k in range(len(MOVES)):
@@ -332,10 +378,10 @@
         scratch_shapes=[
             pltpu.VMEM((L, NSRC, 2 * NPTS), bf16),
             pltpu.VMEM((L, 2 * ROWS, NSRC), bf16),
-            pltpu.VMEM((L, FRQ * PIECE, NPTS), f32),
-            pltpu.VMEM((L, FRQ * PIECE, NPTS), f32),
-            pltpu.VMEM((FRQ * BACK, NPTS), f32),
-            pltpu.VMEM((FRQ * BACK, NPTS), f32),
+            pltpu.VMEM((L, FRQ * PIECE, NPTS), jnp.int32),
+            pltpu.VMEM((L, FRQ * PIECE, NPTS), jnp.int32),
+            pltpu.VMEM((FRQ * BACK, NPTS), jnp.int32),
+            pltpu.VMEM((FRQ * BACK, NPTS), jnp.int32),
             pltpu.VMEM((8, ROWS, NPTS), f32),
             pltpu.VMEM((ROWS, NPTS), jnp.int32),
             pltpu.VMEM((ROWS, NPTS), jnp.int32),

time: 63.5 us -> 60 us (0.945)
  Pallas kernels: 62.6 us -> 59.1 us
    pallas_call x1, Pallas kernels: 62.6 us -> 59.1 us  [per_device(): pl.pallas_call(kernel, out_shape=pltpu.VMEM((8, ROWS, NPTS), f32), in_spe...]
where the time goes in v3:
time: 60 us; the launch traced here: 59.9 us
  Pallas kernels  59.1 us (98%)
  local copies, waits for them, and re-layouts  0.82 us (1%)
    pallas_call x1, Pallas kernels, per_device(): pl.pallas_call(kernel, out_shape=pltpu.VMEM((8, ROWS, NPTS), f32), in_spe...  59.1 us

profile of v3, /device:TPU:1, one launch (start us, length us, event | category | flops | bytes accessed | tf_op | source)
XLA Modules:
  0.0 59.9 jit_solution(13223903602805135433)
XLA Ops:
  0.0 59.1 %marchenko.1 = f32[8,144,128]{2,1,0:T(8,128)S(1)} custom-call(bf16[2,4,144,2304]{3,2,1,0:T(8,128)(2,1)} %refl.1, bf16[2,4,144,128]{3,2,1,0:T(8,128)(2,1)} %focus.1, f32[8,144,128]{2,1,0:T(8,128)} %direct.1, s32[144,128]{1,0:T(8,128)} %onset.1, s32[144,128]{1,0:T(8,128)} %ending.1, f32[128,512]{1,0:T(8,128)} %constant.2.clone.table), custom_call_target="tpu_custom_call" | custom-call | tf_op jit(solution)/shard_map/marchenko/pallas_call | solution.py:373
  59.1 0.8 %copy.8 = f32[8,144,128]{2,1,0:T(8,128)} copy(f32[8,144,128]{2,1,0:T(8,128)S(1)} %marchenko.1) | data formatting | bytes 1179648

commit v4 on v3

--- a/solution.py
+++ b/solution.py
@@ -24,29 +24,33 @@
 LAG = 3
 BACK = (PER + 1) // 2 * 8
 
+PEERS = (10, 11, 8, 9, 6, 14, 7, 15, 4, 12, 5, 13, 2, 3, 1)
 A, B, ALL = (0, 128), (128, 128), (0, 256)
 OWN, PAR = 0, 1
 MOVES = (
-    ("z+", OWN, -1, ALL),
-    ("z+", OWN, -2, ALL),
-    ("z+", OWN, -3, ALL),
-    ("z+", OWN, -4, A),
-    ("z+", PAR, -2, ALL),
-    ("z+", PAR, -3, A),
-    ("z-", OWN, 1, ALL),
-    ("z-", OWN, 2, ALL),
-    ("z-", OWN, 3, ALL),
-    ("z-", OWN, 4, B),
-    ("z-", PAR, 2, ALL),
-    ("z-", PAR, 3, A),
-    ("y", PAR, 0, ALL),
-    ("y", PAR, -1, ALL),
-    ("y", PAR, 1, ALL),
-    ("y", PAR, -3, B),
-    ("y", PAR, 3, B),
-    ("y", PAR, 4, ALL),
+    ("z+", OWN, -1, ALL, 0),
+    ("z+", OWN, -2, ALL, 1),
+    ("z+", OWN, -3, ALL, 2),
+    ("z+", OWN, -4, A, 3),
+    ("z+", PAR, -2, ALL, 5),
+    ("z+", PAR, -3, A, 6),
+    ("z-", OWN, 1, ALL, 0),
+    ("z-", OWN, 2, ALL, 1),
+    ("z-", OWN, 3, ALL, 2),
+    ("z-", OWN, 4, B, 3),
+    ("z-", PAR, 2, ALL, 5),
+    ("z-", PAR, 3, A, 6),
+    ("y", PAR, 0, ALL, 6),
+    ("y", PAR, -1, ALL, 4),
+    ("y", PAR, 1, ALL, 4),
+    ("y", PAR, -3, B, 6),
+    ("y", PAR, 3, B, 6),
+    ("y", PAR, 4, ALL, 6),
 )
 ZP1, ZP2, ZP3, ZP4, ZQ2, ZQ3, ZM1, ZM2, ZM3, ZM4, ZN2, ZN3, Y0, YM1, YP1, YM3, YP3, Y4 = range(18)
+OWN1, OWN2, OWN3, OWN4, PAR1, PAR2, REST = range(7)
+BLOCKS = (2, 2, 2, 1, 2, 2, 4)
+SENT = sum(BLOCKS)
 
 
 def split(value):
@@ -85,7 +89,7 @@
     refl, focus, direct, onset, ending, table,
     out,
     gath, mat, spec, got, trace, back, dir_v, on_v, end_v, tab_v, tab_a, tab_b, early,
-    g_send, g_recv, s_send, s_recv, t_send, t_recv, f_sem, r_sem, loc_sem, own_sem,
+    g_send, g_recv, s_send, s_recv, t_send, t_recv, f_sem, r_sem, loc_sem,
 ):
     s_me, f_me = lax.axis_index("src"), lax.axis_index("freq")
     h, z = s_me // Z, lax.rem(s_me, Z)
@@ -95,68 +99,73 @@
         "y": {"src": (1 - h) * Z + z, "freq": f_me},
     }
 
+    x_me, y_me, c_me = f_me // 4, lax.rem(f_me // 2, 2), lax.rem(f_me, 2)
+
+    def peer_at(d):
+        dx, dy, dc = d // 4, d // 2 % 2, d % 2
+        x = lax.rem(x_me + dx, 4)
+        return (x * 2 + lax.rem(y_me + dy, 2)) * 2 + lax.rem(c_me + dc, 2)
+
+    peers = {d: peer_at(d) for d in PEERS}
+
     def peer(d):
-        return lax.rem(f_me + d, FRQ)
+        return peers[d]
 
     def rows_of(half, offset):
         hh = h if half == OWN else 1 - h
         block = hh * Z + lax.rem(z + offset + Z, Z)
         return pl.ds(pl.multiple_of(block * ROWS, 16), ROWS)
 
-    def move(k, l, receiving):
-        way, half, offset, (lane, width) = MOVES[k]
-        if not receiving:
-            if way == "y":
-                half = 1 - half
-            else:
-                offset = offset + (1 if way == "z+" else -1)
+    def send(k, l):
+        way, half, offset, (lane, width), group = MOVES[k]
+        if way == "y":
+            half = 1 - half
+        else:
+            offset = offset + (1 if way == "z+" else -1)
         ref = gath.at[l, rows_of(half, offset), pl.ds(lane, width)]
-        return pltpu.make_async_remote_copy(
-            src_ref=ref, dst_ref=ref, send_sem=g_send.at[l, k], recv_sem=g_recv.at[l, k],
+        pltpu.make_async_remote_copy(
+            src_ref=ref, dst_ref=ref, send_sem=g_send.at[l], recv_sem=g_recv.at[l, group],
             device_id=targets[way], device_id_type=MESH,
-        )
-
-    def send(k, l):
-        move(k, l, False).start()
-
-    def arrived(k, l):
-        move(k, l, True).wait_recv()
+        ).start()
+
+    def await_all(ref, sem):
+        pltpu.make_async_copy(ref, ref, sem).wait()
+
+    def arrived(group, l):
+        await_all(gath.at[l, pl.ds(0, BLOCKS[group] * ROWS)], g_recv.at[l, group])
 
     mine = pl.ds(pl.multiple_of(s_me * ROWS, 16), ROWS)
 
     def focus_copy(part, l):
         return pltpu.make_async_copy(
-            focus.at[part, l], gath.at[l, mine, pl.ds(part * NPTS, NPTS)], f_sem.at[part, l]
+            focus.at[part, l], gath.at[l, mine, pl.ds(part * NPTS, NPTS)], f_sem
         )
 
     def refl_copy(part, l):
         return pltpu.make_async_copy(
-            refl.at[part, l], mat.at[l, pl.ds(part * ROWS, ROWS)], r_sem.at[part, l]
+            refl.at[part, l], mat.at[l, pl.ds(part * ROWS, ROWS)], r_sem.at[l]
         )
 
     others = [
         pltpu.make_async_copy(a, b, loc_sem.at[i])
         for i, (a, b) in enumerate(((table, tab_v), (onset, on_v), (ending, end_v), (direct, dir_v)))
     ]
+    barrier = pltpu.get_barrier_semaphore()
+    for d in PEERS:
+        pl.semaphore_signal(
+            barrier, inc=1, device_id={"src": s_me, "freq": peer(d)}, device_id_type=MESH
+        )
+    for way in ("y", "z+", "z-"):
+        pl.semaphore_signal(barrier, inc=1, device_id=targets[way], device_id_type=MESH)
     for l in range(L):
         for part in range(2):
             focus_copy(part, l).start()
-
-    barrier = pltpu.get_barrier_semaphore()
-    for way in ("z+", "z-", "y"):
-        pl.semaphore_signal(barrier, inc=1, device_id=targets[way], device_id_type=MESH)
-    for d in range(1, FRQ):
-        pl.semaphore_signal(
-            barrier, inc=1, device_id={"src": s_me, "freq": peer(d)}, device_id_type=MESH
-        )
     for l in range(L):
         for part in range(2):
             refl_copy(part, l).start()
     for c in others:
         c.start()
-    for l in range(L):
-        for part in range(2):
-            focus_copy(part, l).wait()
+    await_all(gath.at[0, pl.ds(0, L * ROWS)], f_sem)
     pl.semaphore_wait(barrier, 3 + FRQ - 1)
 
     def phase(body):
@@ -172,59 +181,45 @@
         send(Y0, l)
 
     def near(l):
-        arrived(ZP1, l)
-        send(ZP2, l)
-        send(YM1, l)
-        arrived(ZM1, l)
-        send(ZM2, l)
-        send(YP1, l)
+        arrived(OWN1, l)
+        for k in (ZP2, ZM2, YM1, YP1):
+            send(k, l)
 
     def second(l):
-        arrived(ZP2, l)
-        send(ZP3, l)
-        arrived(ZM2, l)
-        send(ZM3, l)
+        arrived(OWN2, l)
+        for k in (ZP3, ZM3):
+            send(k, l)
 
     def third(l):
-        arrived(ZP3, l)
-        send(ZP4, l)
-        send(YM3, l)
-        arrived(ZM3, l)
-        send(ZM4, l)
-        send(YP3, l)
-        arrived(YM1, l)
-        send(ZQ2, l)
-        arrived(YP1, l)
-        send(ZN2, l)
+        arrived(OWN3, l)
+        for k in (ZP4, ZM4, YM3, YP3):
+            send(k, l)
+        arrived(PAR1, l)
+        for k in (ZQ2, ZN2):
+            send(k, l)
 
     def fourth(l):
-        arrived(ZP4, l)
-        arrived(ZM4, l)
+        arrived(OWN4, l)
         send(Y4, l)
-        arrived(ZQ2, l)
-        send(ZQ3, l)
-        arrived(ZN2, l)
-        send(ZN3, l)
-
-    def piece_copy(d, l, receiving):
-        to = peer(d)
-        place = peer(FRQ - d) if receiving else f_me
+        arrived(PAR2, l)
+        for k in (ZQ3, ZN3):
+            send(k, l)
+
+    def piece_copy(d, l):
         return pltpu.make_async_remote_copy(
-            src_ref=spec.at[l, pl.ds(pl.multiple_of(to * PIECE, 8), USED)],
-            dst_ref=got.at[l, pl.ds(pl.multiple_of(place * PIECE, 8), USED)],
-            send_sem=s_send.at[l, d], recv_sem=s_recv.at[l, d],
-            device_id={"src": s_me, "freq": to}, device_id_type=MESH,
+            src_ref=spec.at[l, pl.ds(pl.multiple_of(peer(d) * PIECE, 8), USED)],
+            dst_ref=got.at[l, pl.ds(pl.multiple_of(f_me * PIECE, 8), USED)],
+            send_sem=s_send.at[l], recv_sem=s_recv.at[l],
+            device_id={"src": s_me, "freq": peer(d)}, device_id_type=MESH,
         )
 
     def own_piece(l):
         rows = pl.ds(pl.multiple_of(f_me * PIECE, 8), USED)
-        return pltpu.make_async_copy(spec.at[l, rows], got.at[l, rows], own_sem.at[l])
+        return pltpu.make_async_copy(spec.at[l, rows], got.at[l, rows], s_recv.at[l])
 
     def product(l):
-        for k in (Y0, YM3, YP3, ZQ3, ZN3, Y4):
-            arrived(k, l)
-        for part in range(2):
-            refl_copy(part, l).wait()
+        arrived(REST, l)
+        await_all(mat.at[l], r_sem.at[l])
         both = jnp.dot(mat[l], gath[l], preferred_element_type=jnp.float32)
         re = both[:ROWS, :NPTS] - both[ROWS:, NPTS:]
         im = both[:ROWS, NPTS:] + both[ROWS:, :NPTS]
@@ -238,8 +233,8 @@
             for j, word in enumerate(words + [code]):
                 spec[l, pl.ds(p * PIECE + j, 8, stride=PIECE), :] = word
         own_piece(l).start()
-        for d in range(1, FRQ):
-            piece_copy(d, l, False).start()
+        for d in PEERS:
+            piece_copy(d, l).start()
 
     phase(start_own)
     phase(near)
@@ -264,9 +259,7 @@
     lax.fori_loop(0, L + LAG, last, 0)
 
     def collect(l):
-        own_piece(l).wait()
-        for d in range(1, FRQ):
-            piece_copy(d, l, True).wait_recv()
+        await_all(got.at[l, pl.ds(0, FRQ * USED)], s_recv.at[l])
 
     def columns(j, l):
         word = got[l, pl.ds(j, FRQ, stride=PIECE), :]
@@ -309,24 +302,16 @@
         for d in range(FRQ):
             trace[pl.ds(d * BACK + j * 4, 8), :] = word[8 * d : 8 * d + 8]
 
-    def back_copy(d, receiving):
-        to = peer(d)
-        place = peer(FRQ - d) if receiving else f_me
-        return pltpu.make_async_remote_copy(
-            src_ref=trace.at[pl.ds(pl.multiple_of(to * BACK, 8), BACK)],
-            dst_ref=back.at[pl.ds(pl.multiple_of(place * BACK, 8), BACK)],
-            send_sem=t_send.at[d], recv_sem=t_recv.at[d],
-            device_id={"src": s_me, "freq": to}, device_id_type=MESH,
-        )
-
     rows = pl.ds(pl.multiple_of(f_me * BACK, 8), BACK)
-    own_back = pltpu.make_async_copy(trace.at[rows], back.at[rows], own_sem.at[L])
-    for d in range(1, FRQ):
-        back_copy(d, False).start()
-    own_back.start()
-    own_back.wait()
-    for d in range(1, FRQ):
-        back_copy(d, True).wait_recv()
+    for d in PEERS:
+        pltpu.make_async_remote_copy(
+            src_ref=trace.at[pl.ds(pl.multiple_of(peer(d) * BACK, 8), BACK)],
+            dst_ref=back.at[rows],
+            send_sem=t_send, recv_sem=t_recv,
+            device_id={"src": s_me, "freq": peer(d)}, device_id_type=MESH,
+        ).start()
+    pltpu.make_async_copy(trace.at[rows], back.at[rows], t_recv).start()
+    await_all(back, t_recv)
 
     for t in range(8):
         for p in (0, 8):
@@ -340,14 +325,11 @@
                 out[t, r, :] = dir_v[t, r, :] - value * one * two
 
     def sent(l):
-        for k in range(len(MOVES)):
-            move(k, l, False).wait_send()
-        for d in range(1, FRQ):
-            piece_copy(d, l, False).wait_send()
+        await_all(gath.at[l, pl.ds(0, SENT * ROWS)], g_send.at[l])
+        await_all(spec.at[l, pl.ds(0, (FRQ - 1) * USED)], s_send.at[l])
 
     phase(sent)
-    for d in range(1, FRQ):
-        back_copy(d, False).wait_send()
+    await_all(trace.at[pl.ds(0, (FRQ - 1) * BACK)], t_send)
 
 
 def transform_table():
@@ -389,16 +371,15 @@
             pltpu.VMEM((128, 384), bf16),
             pltpu.VMEM((128, 128), bf16),
             pltpu.VMEM((PER, 128, NPTS), f32),
-            dma((L, len(MOVES))),
-            dma((L, len(MOVES))),
-            dma((L, FRQ)),
-            dma((L, FRQ)),
-            dma((FRQ,)),
-            dma((FRQ,)),
-            dma((2, L)),
-            dma((2, L)),
+            dma((L,)),
+            dma((L, len(BLOCKS))),
+            dma((L,)),
+            dma((L,)),
+            dma,
+            dma,
+            dma,
+            dma((L,)),
             dma((4,)),
-            dma((L + 1,)),
         ],
         compiler_params=pltpu.CompilerParams(
             collective_id=0, has_side_effects=True, vmem_limit_bytes=60 * 2**20

time: 60 us -> 56.6 us (0.943)
  Pallas kernels: 59.1 us -> 55.8 us
    pallas_call x1, Pallas kernels: 59.1 us -> 55.8 us  [per_device(): pl.pallas_call(kernel, out_shape=pltpu.VMEM((8, ROWS, NPTS), f32), in_spe...]
where the time goes in v4:
time: 56.6 us
  Pallas kernels  55.8 us (99%)
  local copies, waits for them, and re-layouts  0.82 us (1%)
    pallas_call x1, Pallas kernels, per_device(): pl.pallas_call(kernel, out_shape=pltpu.VMEM((8, ROWS, NPTS), f32), in_spe...  55.8 us

profile of v4, /device:TPU:1, one launch (start us, length us, event | category | flops | bytes accessed | tf_op | source)
XLA Modules:
  0.0 56.6 jit_solution(4383500984143169181)
XLA Ops:
  0.0 55.8 %marchenko.1 = f32[8,144,128]{2,1,0:T(8,128)S(1)} custom-call(bf16[2,4,144,2304]{3,2,1,0:T(8,128)(2,1)} %refl.1, bf16[2,4,144,128]{3,2,1,0:T(8,128)(2,1)} %focus.1, f32[8,144,128]{2,1,0:T(8,128)} %direct.1, s32[144,128]{1,0:T(8,128)} %onset.1, s32[144,128]{1,0:T(8,128)} %ending.1, f32[128,512]{1,0:T(8,128)} %constant.2.clone.table), custom_call_target="tpu_custom_call" | custom-call | tf_op jit(solution)/shard_map/marchenko/pallas_call | solution.py:355
  55.8 0.8 %copy.8 = f32[8,144,128]{2,1,0:T(8,128)} copy(f32[8,144,128]{2,1,0:T(8,128)S(1)} %marchenko.1) | data formatting | bytes 1179648

commit v5 on v4

--- a/solution.py
+++ b/solution.py
@@ -124,7 +124,7 @@
             offset = offset + (1 if way == "z+" else -1)
         ref = gath.at[l, rows_of(half, offset), pl.ds(lane, width)]
         pltpu.make_async_remote_copy(
-            src_ref=ref, dst_ref=ref, send_sem=g_send.at[l], recv_sem=g_recv.at[l, group],
+            src_ref=ref, dst_ref=ref, send_sem=g_send, recv_sem=g_recv.at[l, group],
             device_id=targets[way], device_id_type=MESH,
         ).start()
 
@@ -143,7 +143,7 @@
 
     def refl_copy(part, l):
         return pltpu.make_async_copy(
-            refl.at[part, l], mat.at[l, pl.ds(part * ROWS, ROWS)], r_sem.at[l]
+            refl.at[part, l], mat.at[l, pl.ds(part * ROWS, ROWS)], r_sem
         )
 
     others = [
@@ -209,7 +209,7 @@
         return pltpu.make_async_remote_copy(
             src_ref=spec.at[l, pl.ds(pl.multiple_of(peer(d) * PIECE, 8), USED)],
             dst_ref=got.at[l, pl.ds(pl.multiple_of(f_me * PIECE, 8), USED)],
-            send_sem=s_send.at[l], recv_sem=s_recv.at[l],
+            send_sem=s_send, recv_sem=s_recv.at[l],
             device_id={"src": s_me, "freq": peer(d)}, device_id_type=MESH,
         )
 
@@ -219,7 +219,6 @@
 
     def product(l):
         arrived(REST, l)
-        await_all(mat.at[l], r_sem.at[l])
         both = jnp.dot(mat[l], gath[l], preferred_element_type=jnp.float32)
         re = both[:ROWS, :NPTS] - both[ROWS:, NPTS:]
         im = both[:ROWS, NPTS:] + both[ROWS:, :NPTS]
@@ -240,6 +239,7 @@
     phase(near)
     phase(second)
     phase(third)
+    await_all(mat, r_sem)
     for c in others:
         c.wait()
     tab_a[...] = tab_v[:, :384].astype(jnp.bfloat16)
@@ -311,7 +311,7 @@
             device_id={"src": s_me, "freq": peer(d)}, device_id_type=MESH,
         ).start()
     pltpu.make_async_copy(trace.at[rows], back.at[rows], t_recv).start()
-    await_all(back, t_recv)
+    await_all(back.at[pl.ds(0, FRQ * BACK)], t_recv)
 
     for t in range(8):
         for p in (0, 8):
@@ -324,11 +324,8 @@
                 r = pl.ds(16 * j + p, 8)
                 out[t, r, :] = dir_v[t, r, :] - value * one * two
 
-    def sent(l):
-        await_all(gath.at[l, pl.ds(0, SENT * ROWS)], g_send.at[l])
-        await_all(spec.at[l, pl.ds(0, (FRQ - 1) * USED)], s_send.at[l])
-
-    phase(sent)
+    await_all(gath.at[:, pl.ds(0, SENT * ROWS)], g_send)
+    await_all(spec.at[:, pl.ds(0, (FRQ - 1) * USED)], s_send)
     await_all(trace.at[pl.ds(0, (FRQ - 1) * BACK)], t_send)
 
 
@@ -360,10 +357,10 @@
         scratch_shapes=[
             pltpu.VMEM((L, NSRC, 2 * NPTS), bf16),
             pltpu.VMEM((L, 2 * ROWS, NSRC), bf16),
-            pltpu.VMEM((L, FRQ * PIECE, NPTS), jnp.int32),
-            pltpu.VMEM((L, FRQ * PIECE, NPTS), jnp.int32),
-            pltpu.VMEM((FRQ * BACK, NPTS), jnp.int32),
-            pltpu.VMEM((FRQ * BACK, NPTS), jnp.int32),
+            pltpu.VMEM((L, (FRQ + 1) * PIECE, NPTS), jnp.int32),
+            pltpu.VMEM((L, (FRQ + 1) * PIECE, NPTS), jnp.int32),
+            pltpu.VMEM(((FRQ + 1) * BACK, NPTS), jnp.int32),
+            pltpu.VMEM(((FRQ + 1) * BACK, NPTS), jnp.int32),
             pltpu.VMEM((8, ROWS, NPTS), f32),
             pltpu.VMEM((ROWS, NPTS), jnp.int32),
             pltpu.VMEM((ROWS, NPTS), jnp.int32),
@@ -371,14 +368,14 @@
             pltpu.VMEM((128, 384), bf16),
             pltpu.VMEM((128, 128), bf16),
             pltpu.VMEM((PER, 128, NPTS), f32),
+            dma,
+            dma((L, len(BLOCKS))),
+            dma,
             dma((L,)),
-            dma((L, len(BLOCKS))),
-            dma((L,)),
-            dma((L,)),
-            dma,
-            dma,
-            dma,
-            dma((L,)),
+            dma,
+            dma,
+            dma,
+            dma,
             dma((4,)),
         ],
         compiler_params=pltpu.CompilerParams(

time: 56.6 us -> 56.5 us (level)
  no operation moved by 1% of the time
where the time goes in v5:
time: 56.5 us
  Pallas kernels  55.6 us (98%)
  local copies, waits for them, and re-layouts  0.82 us (1%)
    pallas_call x1, Pallas kernels, per_device(): pl.pallas_call(kernel, out_shape=pltpu.VMEM((8, ROWS, NPTS), f32), in_spe...  55.6 us

profile of v5, /device:TPU:1, one launch (start us, length us, event | category | flops | bytes accessed | tf_op | source)
XLA Modules:
  0.0 56.5 jit_solution(6609346280400933430)
XLA Ops:
  0.0 55.6 %marchenko.1 = f32[8,144,128]{2,1,0:T(8,128)S(1)} custom-call(bf16[2,4,144,2304]{3,2,1,0:T(8,128)(2,1)} %refl.1, bf16[2,4,144,128]{3,2,1,0:T(8,128)(2,1)} %focus.1, f32[8,144,128]{2,1,0:T(8,128)} %direct.1, s32[144,128]{1,0:T(8,128)} %onset.1, s32[144,128]{1,0:T(8,128)} %ending.1, f32[128,512]{1,0:T(8,128)} %constant.2.clone.table), custom_call_target="tpu_custom_call" | custom-call | tf_op jit(solution)/shard_map/marchenko/pallas_call | solution.py:352
  55.6 0.8 %copy.8 = f32[8,144,128]{2,1,0:T(8,128)} copy(f32[8,144,128]{2,1,0:T(8,128)S(1)} %marchenko.1) | data formatting | bytes 1179648

commit v6 on v5

--- a/solution.py
+++ b/solution.py
@@ -24,7 +24,7 @@
 LAG = 3
 BACK = (PER + 1) // 2 * 8
 
-PEERS = (10, 11, 8, 9, 6, 14, 7, 15, 4, 12, 5, 13, 2, 3, 1)
+PEERS = (10, 6, 14, 11, 7, 15, 8, 4, 12, 9, 5, 13, 2, 3, 1)
 A, B, ALL = (0, 128), (128, 128), (0, 256)
 OWN, PAR = 0, 1
 MOVES = (

time: 56.5 us -> 56.3 us (level)
  no operation moved by 1% of the time
where the time goes in v6:
time: 56.3 us; the launch traced here: 56.2 us
  Pallas kernels  55.4 us (98%)
  local copies, waits for them, and re-layouts  0.82 us (1%)
    pallas_call x1, Pallas kernels, per_device(): pl.pallas_call(kernel, out_shape=pltpu.VMEM((8, ROWS, NPTS), f32), in_spe...  55.4 us

profile of v6, /device:TPU:1, one launch (start us, length us, event | category | flops | bytes accessed | tf_op | source)
XLA Modules:
  0.0 56.2 jit_solution(8702888748755679225)
XLA Ops:
  0.0 55.4 %marchenko.1 = f32[8,144,128]{2,1,0:T(8,128)S(1)} custom-call(bf16[2,4,144,2304]{3,2,1,0:T(8,128)(2,1)} %refl.1, bf16[2,4,144,128]{3,2,1,0:T(8,128)(2,1)} %focus.1, f32[8,144,128]{2,1,0:T(8,128)} %direct.1, s32[144,128]{1,0:T(8,128)} %onset.1, s32[144,128]{1,0:T(8,128)} %ending.1, f32[128,512]{1,0:T(8,128)} %constant.2.clone.table), custom_call_target="tpu_custom_call" | custom-call | tf_op jit(solution)/shard_map/marchenko/pallas_call | solution.py:352
  55.4 0.8 %copy.8 = f32[8,144,128]{2,1,0:T(8,128)} copy(f32[8,144,128]{2,1,0:T(8,128)S(1)} %marchenko.1) | data formatting | bytes 1179648

commit v7 on v6

--- a/solution.py
+++ b/solution.py
@@ -21,11 +21,12 @@
 PER = ROWS // FRQ
 PIECE = 24
 USED = PER + 1
-LAG = 3
+LAG = 4
 BACK = (PER + 1) // 2 * 8
 
 PEERS = (10, 6, 14, 11, 7, 15, 8, 4, 12, 9, 5, 13, 2, 3, 1)
-A, B, ALL = (0, 128), (128, 128), (0, 256)
+A, B, ALL = (0, 144, 0, 128), (0, 144, 128, 128), (0, 144, 0, 256)
+TOP, LOW = (0, 80, 0, 256), (80, 64, 0, 256)
 OWN, PAR = 0, 1
 MOVES = (
     ("z+", OWN, -1, ALL, 0),
@@ -33,18 +34,18 @@
     ("z+", OWN, -3, ALL, 2),
     ("z+", OWN, -4, A, 3),
     ("z+", PAR, -2, ALL, 5),
-    ("z+", PAR, -3, A, 6),
+    ("z+", PAR, -3, TOP, 6),
     ("z-", OWN, 1, ALL, 0),
     ("z-", OWN, 2, ALL, 1),
     ("z-", OWN, 3, ALL, 2),
     ("z-", OWN, 4, B, 3),
     ("z-", PAR, 2, ALL, 5),
-    ("z-", PAR, 3, A, 6),
+    ("z-", PAR, 3, TOP, 6),
     ("y", PAR, 0, ALL, 6),
     ("y", PAR, -1, ALL, 4),
     ("y", PAR, 1, ALL, 4),
-    ("y", PAR, -3, B, 6),
-    ("y", PAR, 3, B, 6),
+    ("y", PAR, -3, LOW, 6),
+    ("y", PAR, 3, LOW, 6),
     ("y", PAR, 4, ALL, 6),
 )
 ZP1, ZP2, ZP3, ZP4, ZQ2, ZQ3, ZM1, ZM2, ZM3, ZM4, ZN2, ZN3, Y0, YM1, YP1, YM3, YP3, Y4 = range(18)
@@ -111,18 +112,18 @@
     def peer(d):
         return peers[d]
 
-    def rows_of(half, offset):
+    def rows_of(half, offset, first, count):
         hh = h if half == OWN else 1 - h
         block = hh * Z + lax.rem(z + offset + Z, Z)
-        return pl.ds(pl.multiple_of(block * ROWS, 16), ROWS)
+        return pl.ds(pl.multiple_of(block * ROWS + first, 16), count)
 
     def send(k, l):
-        way, half, offset, (lane, width), group = MOVES[k]
+        way, half, offset, (first, count, lane, width), group = MOVES[k]
         if way == "y":
             half = 1 - half
         else:
             offset = offset + (1 if way == "z+" else -1)
-        ref = gath.at[l, rows_of(half, offset), pl.ds(lane, width)]
+        ref = gath.at[l, rows_of(half, offset, first, count), pl.ds(lane, width)]
         pltpu.make_async_remote_copy(
             src_ref=ref, dst_ref=ref, send_sem=g_send, recv_sem=g_recv.at[l, group],
             device_id=targets[way], device_id_type=MESH,

time: 56.3 us -> 56.3 us (level)
  no operation moved by 1% of the time
where the time goes in v7:
time: 56.3 us; the launch traced here: 56.2 us
  Pallas kernels  55.4 us (98%)
  local copies, waits for them, and re-layouts  0.82 us (1%)
    pallas_call x1, Pallas kernels, per_device(): pl.pallas_call(kernel, out_shape=pltpu.VMEM((8, ROWS, NPTS), f32), in_spe...  55.4 us

profile of v7, /device:TPU:1, one launch (start us, length us, event | category | flops | bytes accessed | tf_op | source)
XLA Modules:
  0.0 56.2 jit_solution(16219271287334855882)
XLA Ops:
  0.0 55.4 %marchenko.1 = f32[8,144,128]{2,1,0:T(8,128)S(1)} custom-call(bf16[2,4,144,2304]{3,2,1,0:T(8,128)(2,1)} %refl.1, bf16[2,4,144,128]{3,2,1,0:T(8,128)(2,1)} %focus.1, f32[8,144,128]{2,1,0:T(8,128)} %direct.1, s32[144,128]{1,0:T(8,128)} %onset.1, s32[144,128]{1,0:T(8,128)} %ending.1, f32[128,512]{1,0:T(8,128)} %constant.2.clone.table), custom_call_target="tpu_custom_call" | custom-call | tf_op jit(solution)/shard_map/marchenko/pallas_call | solution.py:353
  55.4 0.8 %copy.8 = f32[8,144,128]{2,1,0:T(8,128)} copy(f32[8,144,128]{2,1,0:T(8,128)S(1)} %marchenko.1) | data formatting | bytes 1179648
